TPU v7x, 32 devices: a whole 2x2x4 slice. The times are simulated.
32 devices in a mesh: inline: 16 (over z, y, core), chan: 2 (over x).
Axes of the slice: x: 2, y: 2, z: 4, core: 2. Of those that a mesh axis runs over, the one named last changes fastest.
Arguments:
- inputs: bfloat16 [48, 4, 64, 256], P('inline', 'chan'), may hold values from -6 to 6
- w_in: bfloat16 [256, 256], replicated, may hold values from -0.375 to 0.375
- w_group: bfloat16 [27, 8, 256], replicated, may hold values from -0.4375 to 0.4375
- w_out: bfloat16 [256, 256], replicated, may hold values from -0.375 to 0.375
- cotangent: bfloat16 [48, 4, 64, 256], P('inline', 'chan'), may hold values from -6 to 6
Outputs:
- outputs: bfloat16 [48, 4, 64, 256], P('inline', 'chan')
- input_grad: bfloat16 [48, 4, 64, 256], P('inline', 'chan')
- grad_w_in: float32 [256, 256], replicated
- grad_group: float32 [27, 8, 256], replicated
- grad_w_out: float32 [256, 256], replicated
All inputs are finite; a program needn't handle non-finite values.
Results may differ from a plain program's by a relative error of at most 0.0056.
Values may be sent and summed in bfloat16 or wider, within the bound.
A program may use at most 64 MiB of HBM per device.

v0:
```python
import jax
import jax.numpy as jnp
from jax import lax
from jax.sharding import PartitionSpec as P

GW = 8


def extended_2(array, sides, width):
    for axis, dim in sides:
        peers, length = (lax.axis_size(axis), array.shape[dim])
        up = [(i, (i + 1) % peers) for i in range(peers - 1)]
        down = [(j, i) for i, j in up]
        last = lax.slice_in_dim(array, length - width, length, axis=dim)
        leading = lax.slice_in_dim(array, 0, width, axis=dim)
        before = lax.ppermute(last, axis, up)
        after = lax.ppermute(leading, axis, down)
        array = jnp.concatenate([before, array, after], axis=dim)
    return array


def swish(value):
    return value * jax.nn.sigmoid(value)


def swish_slope(value):
    sig = jax.nn.sigmoid(value)
    return sig * (1.0 + value * (1.0 - sig))


def tap_stack(padded, aa, rows, cross, depth, tiles, tile, flipped):
    pieces = []
    for bb in range(3):
        for cc in range(3):
            if flipped:
                begin_a, begin_b, begin_c = (2 - aa, 2 - bb, 2 - cc)
            else:
                begin_a, begin_b, begin_c = (aa, bb, cc)
            piece = padded[
                begin_a : begin_a + rows, begin_b : begin_b + cross, begin_c : begin_c + depth
            ]
            pieces.append(piece.reshape(rows * cross * depth, tiles, tile))
    return jnp.stack(pieces)


def extend_forward(field):
    return extended_2(field, (("inline", 0), ("chan", 1)), 1)


def extend_backward(field):
    return extended_2(field, (("inline", 0), ("chan", 1)), 1)


def shards(inputs, w_in, w_group, w_out, cotangent):
    rows, cross, depth, channels = inputs.shape
    tile = min(channels, 128)
    tiles = channels // tile
    cells = rows * cross * depth
    block_mask = jnp.arange(tile)[:, None] // GW == jnp.arange(tile)[None, :] // GW
    spread = jnp.tile(w_group.reshape(27, GW, tiles, tile), (1, tile // GW, 1, 1))
    dense = jnp.where(
        block_mask[None, None], jnp.transpose(spread, (0, 2, 1, 3)), jnp.zeros((), jnp.bfloat16)
    )
    in_flat = inputs.reshape(cells, channels)
    pre_one = jnp.dot(in_flat, w_in, preferred_element_type=jnp.float32)
    first = swish(pre_one).astype(jnp.bfloat16)
    extended = extend_forward(first.reshape(rows, cross, depth, channels))
    padded_one = jnp.pad(extended, ((0, 0), (0, 0), (1, 1), (0, 0)))
    conv = jnp.zeros((cells, tiles, tile), jnp.float32)
    for aa in range(3):
        stacked = tap_stack(padded_one, aa, rows, cross, depth, tiles, tile, False)
        conv = conv + jnp.einsum(
            "tnki,tkio->nko",
            stacked,
            dense[9 * aa : 9 * aa + 9],
            preferred_element_type=jnp.float32,
        )
    conv_flat = conv.reshape(cells, channels)
    second = swish(conv_flat).astype(jnp.bfloat16)
    mixed_two = jnp.dot(second, w_out, preferred_element_type=jnp.float32)
    outputs = (
        (in_flat.astype(jnp.float32) + mixed_two)
        .astype(jnp.bfloat16)
        .reshape(rows, cross, depth, channels)
    )
    cot_flat = cotangent.reshape(cells, channels)
    back_two = jnp.einsum("no,co->nc", cot_flat, w_out, preferred_element_type=jnp.float32)
    grad_out = jnp.einsum("nc,no->co", second, cot_flat, preferred_element_type=jnp.float32)
    grad_conv = (back_two * swish_slope(conv_flat)).astype(jnp.bfloat16)
    extended_two = extend_backward(grad_conv.reshape(rows, cross, depth, channels))
    padded_two = jnp.pad(extended_two, ((0, 0), (0, 0), (1, 1), (0, 0)))
    grad_split = grad_conv.reshape(cells, tiles, tile)
    back_one = jnp.zeros((cells, tiles, tile), jnp.float32)
    grad_parts = []
    for aa in range(3):
        flipped = tap_stack(padded_two, aa, rows, cross, depth, tiles, tile, True)
        back_one = back_one + jnp.einsum(
            "tnko,tkio->nki",
            flipped,
            dense[9 * aa : 9 * aa + 9],
            preferred_element_type=jnp.float32,
        )
        stacked = tap_stack(padded_one, aa, rows, cross, depth, tiles, tile, False)
        grad_parts.append(
            jnp.einsum("tnki,nko->tkio", stacked, grad_split, preferred_element_type=jnp.float32)
        )
    grad_dense = jnp.concatenate(grad_parts, axis=0) * block_mask[None, None].astype(jnp.float32)
    grad_folded = jnp.sum(grad_dense.reshape(27, tiles, tile // GW, GW, tile), axis=2)
    grad_local = jnp.transpose(grad_folded, (0, 2, 1, 3)).reshape(27, GW, channels)
    grad_mixed = (back_one.reshape(cells, channels) * swish_slope(pre_one)).astype(jnp.bfloat16)
    back_in = jnp.einsum("no,co->nc", grad_mixed, w_in, preferred_element_type=jnp.float32)
    input_grad = (
        (cot_flat.astype(jnp.float32) + back_in)
        .astype(jnp.bfloat16)
        .reshape(rows, cross, depth, channels)
    )
    grad_in = jnp.einsum("nc,no->co", in_flat, grad_mixed, preferred_element_type=jnp.float32)
    summed_in, summed_group, summed_out = lax.psum(
        (grad_in, grad_local, grad_out), ("inline", "chan")
    )
    return (outputs, input_grad, summed_in, summed_group, summed_out)


def solution(mesh):
    in_specs = (P("inline", "chan", None, None), P(), P(), P(), P("inline", "chan", None, None))
    out_specs = (P("inline", "chan", None, None), P("inline", "chan", None, None), P(), P(), P())
    return jax.shard_map(shards, mesh=mesh, in_specs=in_specs, out_specs=out_specs, check_vma=False)
```

profile of v0, /device:TPU:0, one launch (start us, length us, event | category | flops | bytes accessed | tf_op | source)
XLA Modules:
  0.0 300.9 jit_solution(14191217393172015019)
XLA Ops:
  8.1 1.9 multiply_convert_fusion.2
  11.3 3.0 %collective-permute-start = (bf16[1,2,64,256]{3,2,1,0:T(8,128)(2,1)S(1)}, bf16[1,2,64,256]{3,2,1,0:T(8,128)(2,1)S(1)}, u32[]{:S(2)}, u32[]{:S(2)}) collective-permute-start(bf16[1,2,64,256]{3,2,1,0:T(8,128)(2,1)S(1)} %bitcast.292), channel_id=1, source_target_pairs={{0,2},{2,4},{4,6},{6,8},{8,10},{10,12},{12,14},{14,16},{16,18},{18... | collective-permute-start | bytes 196616 | tf_op jit(solution)/shard_map/ppermute | solution.py:16
  16.6 4.9 %collective-permute-start.2 = (bf16[5,1,64,256]{3,2,1,0:T(8,128)(2,1)S(1)}, bf16[5,1,64,256]{3,2,1,0:T(8,128)(2,1)S(1)}, u32[]{:S(2)}, u32[]{:S(2)}) collective-permute-start(bf16[5,1,64,256]{3,2,1,0:T(8,128)(2,1)S(1)} %get-tuple-element.82), channel_id=1, source_target_pairs={{0,1},{2,3},{4,5},{6,7},{8,9},{10,11},{12,13},{14,15},{16,17},{18,... | collective-permute-start | bytes 491528 | tf_op jit(solution)/shard_map/ppermute | solution.py:16
  23.6 2.8 copy.159
  27.9 2.4 collective-permute-done.3
  37.4 1.7 stack_reshape.215
  39.1 1.7 stack_reshape.213
  42.4 1.7 stack_reshape.210
  44.1 1.7 stack_reshape.209
  66.1 4.0 %copy.220 = bf16[9,384,2,128]{1,3,0,2:T(8,128)(2,1)} copy(bf16[9,384,2,128]{3,1,0,2:T(8,128)(2,1)} %copy_dynamic-update-slice_fusion.45) | data formatting | bytes 3538944 | tf_op jit(solution)/shard_map/stack | solution.py:43
  76.5 3.9 %copy.222 = bf16[9,384,2,128]{1,3,0,2:T(8,128)(2,1)} copy(bf16[9,384,2,128]{3,1,0,2:T(8,128)(2,1)} %copy_dynamic-update-slice_fusion.36) | data formatting | bytes 3538944 | tf_op jit(solution)/shard_map/stack | solution.py:43
  80.4 2.1 fusion.23
  82.5 2.2 fusion.35
  91.2 3.9 %copy.224 = bf16[9,384,2,128]{1,3,0,2:T(8,128)(2,1)} copy(bf16[9,384,2,128]{3,1,0,2:T(8,128)(2,1)} %copy_dynamic-update-slice_fusion.27) | data formatting | bytes 3538944 | tf_op jit(solution)/shard_map/stack | solution.py:43
  95.1 2.2 fusion.52
  103.1 3.0 %collective-permute-start.4 = (bf16[1,2,64,256]{3,2,1,0:T(8,128)(2,1)S(1)}, bf16[1,2,64,256]{3,2,1,0:T(8,128)(2,1)S(1)}, u32[]{:S(2)}, u32[]{:S(2)}) collective-permute-start(bf16[1,2,64,256]{3,2,1,0:T(8,128)(2,1)S(1)} %bitcast.290), channel_id=1, source_target_pairs={{0,2},{2,4},{4,6},{6,8},{8,10},{10,12},{12,14},{14,16},{16,18},{18... | collective-permute-start | bytes 196616 | tf_op jit(solution)/shard_map/ppermute | solution.py:16
  107.6 2.2 collective-permute-start.6
  114.2 3.3 %collective-permute-done.7 = bf16[5,1,64,256]{3,2,1,0:T(8,128)(2,1)S(1)} collective-permute-done((bf16[5,1,64,256]{3,2,1,0:T(8,128)(2,1)S(1)}, bf16[5,1,64,256]{3,2,1,0:T(8,128)(2,1)S(1)}, u32[]{:S(2)}, u32[]{:S(2)}) %collective-permute-start.7) | collective-permute-done | bytes 163872 | tf_op jit(solution)/shard_map/ppermute | solution.py:17
  127.1 1.7 stack_reshape.240
  130.5 1.7 stack_reshape.237
  137.1 1.7 stack_reshape.231
  157.2 131.8 %all-reduce.5.cloned.1.call-done = (f32[256,256]{0,1:T(8,128)}, f32[27,8,256]{2,1,0:T(8,128)}, f32[256,256]{1,0:T(8,128)}) async-done(((f32[256,256]{0,1:T(8,128)}, f32[27,8,256]{2,1,0:T(8,128)}, f32[256,256]{1,0:T(8,128)}), (f32[256,256]{0,1:T(8,128)}, f32[27,8,256]{2,1,0:T(8,128)}, f32[256,256]{1,0:T(8,128)})) %all-reduce.5.cloned.1.call-update) | async-done | bytes 745488 | tf_op jit(solution)/shard_map/psum | solution.py:118
  289.0 1.8 copy.226
  292.4 1.7 copy.358
  (278 shorter events, 97.2 us)
Async XLA Ops:
  7.2 7.2 %copy-start.60 = (bf16[27,8,256]{2,1,0:T(8,128)(2,1)S(1)}, bf16[27,8,256]{2,1,0:T(8,128)(2,1)}, u32[]{:S(2)}) copy-start(bf16[27,8,256]{2,1,0:T(8,128)(2,1)} %param.7) | copy-start | bytes 331780
  7.2 281.8 %all-reduce.5.cloned.1.call-start = ((), (), s32[]{:S(2)}) async-start(), calls=%async_computation | async-start | bytes 1490944 | tf_op jit(solution)/shard_map/psum | solution.py:118
  10.0 6.5 %collective-permute-start.1 = (bf16[1,2,64,256]{3,2,1,0:T(8,128)(2,1)S(1)}, bf16[1,2,64,256]{3,2,1,0:T(8,128)(2,1)S(1)}, u32[]{:S(2)}, u32[]{:S(2)}) collective-permute-start(bf16[1,2,64,256]{3,2,1,0:T(8,128)(2,1)S(1)} %bitcast.293), channel_id=1, source_target_pairs={{2,0},{4,2},{6,4},{8,6},{10,8},{12,10},{14,12},{16,14},{18,16},{20... | collective-permute-start | bytes 196616 | tf_op jit(solution)/shard_map/ppermute | solution.py:17
  11.3 5.2 %collective-permute-start = (bf16[1,2,64,256]{3,2,1,0:T(8,128)(2,1)S(1)}, bf16[1,2,64,256]{3,2,1,0:T(8,128)(2,1)S(1)}, u32[]{:S(2)}, u32[]{:S(2)}) collective-permute-start(bf16[1,2,64,256]{3,2,1,0:T(8,128)(2,1)S(1)} %bitcast.292), channel_id=1, source_target_pairs={{0,2},{2,4},{4,6},{6,8},{8,10},{10,12},{12,14},{14,16},{16,18},{18... | collective-permute-start | bytes 196616 | tf_op jit(solution)/shard_map/ppermute | solution.py:16
  16.6 11.3 %collective-permute-start.2 = (bf16[5,1,64,256]{3,2,1,0:T(8,128)(2,1)S(1)}, bf16[5,1,64,256]{3,2,1,0:T(8,128)(2,1)S(1)}, u32[]{:S(2)}, u32[]{:S(2)}) collective-permute-start(bf16[5,1,64,256]{3,2,1,0:T(8,128)(2,1)S(1)} %get-tuple-element.82), channel_id=1, source_target_pairs={{0,1},{2,3},{4,5},{6,7},{8,9},{10,11},{12,13},{14,15},{16,17},{18,... | collective-permute-start | bytes 491528 | tf_op jit(solution)/shard_map/ppermute | solution.py:16
  21.5 8.9 %collective-permute-start.3 = (bf16[5,1,64,256]{3,2,1,0:T(8,128)(2,1)S(1)}, bf16[5,1,64,256]{3,2,1,0:T(8,128)(2,1)S(1)}, u32[]{:S(2)}, u32[]{:S(2)}) collective-permute-start(bf16[5,1,64,256]{3,2,1,0:T(8,128)(2,1)S(1)} %get-tuple-element.83), channel_id=1, source_target_pairs={{1,0},{3,2},{5,4},{7,6},{9,8},{11,10},{13,12},{15,14},{17,16},{19,... | collective-permute-start | bytes 491528 | tf_op jit(solution)/shard_map/ppermute | solution.py:17
  55.5 7.0 %copy-start.18 = (bf16[1,384,2,128]{3,2,1,0:T(2,128)(2,1)S(1)}, bf16[1,384,2,128]{3,2,1,0:T(2,128)(2,1)}, u32[]{:S(2)}) copy-start(bf16[1,384,2,128]{3,2,1,0:T(2,128)(2,1)} %stack_reshape.193) | copy-start | bytes 589828
  56.3 7.6 %copy-start.46 = (bf16[1,384,2,128]{3,2,1,0:T(2,128)(2,1)S(1)}, bf16[1,384,2,128]{3,2,1,0:T(2,128)(2,1)}, u32[]{:S(2)}) copy-start(bf16[1,384,2,128]{3,2,1,0:T(2,128)(2,1)} %stack_reshape.195) | copy-start | bytes 589828
  57.1 7.6 %copy-start.28 = (bf16[1,384,2,128]{3,2,1,0:T(2,128)(2,1)S(1)}, bf16[1,384,2,128]{3,2,1,0:T(2,128)(2,1)}, u32[]{:S(2)}) copy-start(bf16[1,384,2,128]{3,2,1,0:T(2,128)(2,1)} %stack_reshape.196) | copy-start | bytes 589828
  66.1 4.7 %copy-start.25 = (bf16[1,384,2,128]{3,2,1,0:T(2,128)(2,1)S(1)}, bf16[1,384,2,128]{3,2,1,0:T(2,128)(2,1)}, u32[]{:S(2)}) copy-start(bf16[1,384,2,128]{3,2,1,0:T(2,128)(2,1)} %stack_reshape.199) | copy-start | bytes 589828
  66.1 5.4 %copy-start.43 = (bf16[1,384,2,128]{3,2,1,0:T(2,128)(2,1)S(1)}, bf16[1,384,2,128]{3,2,1,0:T(2,128)(2,1)}, u32[]{:S(2)}) copy-start(bf16[1,384,2,128]{3,2,1,0:T(2,128)(2,1)} %stack_reshape.200) | copy-start | bytes 589828
  66.1 6.1 %copy-start.41 = (bf16[1,384,2,128]{3,2,1,0:T(2,128)(2,1)S(1)}, bf16[1,384,2,128]{3,2,1,0:T(2,128)(2,1)}, u32[]{:S(2)}) copy-start(bf16[1,384,2,128]{3,2,1,0:T(2,128)(2,1)} %stack_reshape.201) | copy-start | bytes 589828
  66.1 6.8 %copy-start.9 = (bf16[1,384,2,128]{3,2,1,0:T(2,128)(2,1)S(1)}, bf16[1,384,2,128]{3,2,1,0:T(2,128)(2,1)}, u32[]{:S(2)}) copy-start(bf16[1,384,2,128]{3,2,1,0:T(2,128)(2,1)} %stack_reshape.202) | copy-start | bytes 589828
  70.1 5.0 %copy-start.13 = (bf16[1,384,2,128]{3,2,1,0:T(2,128)(2,1)S(1)}, bf16[1,384,2,128]{3,2,1,0:T(2,128)(2,1)}, u32[]{:S(2)}) copy-start(bf16[1,384,2,128]{3,2,1,0:T(2,128)(2,1)} %stack_reshape.205) | copy-start | bytes 589828
  70.1 5.7 %copy-start.32 = (bf16[1,384,2,128]{3,2,1,0:T(2,128)(2,1)S(1)}, bf16[1,384,2,128]{3,2,1,0:T(2,128)(2,1)}, u32[]{:S(2)}) copy-start(bf16[1,384,2,128]{3,2,1,0:T(2,128)(2,1)} %stack_reshape.206) | copy-start | bytes 589828
  82.5 4.4 %copy-start.23 = (bf16[1,384,2,128]{3,2,1,0:T(2,128)(2,1)S(1)}, bf16[1,384,2,128]{3,2,1,0:T(2,128)(2,1)}, u32[]{:S(2)}) copy-start(bf16[1,384,2,128]{3,2,1,0:T(2,128)(2,1)} %stack_reshape.210) | copy-start | bytes 589828
  82.5 5.1 %copy-start.4 = (bf16[1,384,2,128]{3,2,1,0:T(2,128)(2,1)S(1)}, bf16[1,384,2,128]{3,2,1,0:T(2,128)(2,1)}, u32[]{:S(2)}) copy-start(bf16[1,384,2,128]{3,2,1,0:T(2,128)(2,1)} %stack_reshape.211) | copy-start | bytes 589828
  84.8 5.0 %copy-start.7 = (bf16[1,384,2,128]{3,2,1,0:T(2,128)(2,1)S(1)}, bf16[1,384,2,128]{3,2,1,0:T(2,128)(2,1)}, u32[]{:S(2)}) copy-start(bf16[1,384,2,128]{3,2,1,0:T(2,128)(2,1)} %stack_reshape.214) | copy-start | bytes 589828
  84.8 5.7 %copy-start.14 = (bf16[1,384,2,128]{3,2,1,0:T(2,128)(2,1)S(1)}, bf16[1,384,2,128]{3,2,1,0:T(2,128)(2,1)}, u32[]{:S(2)}) copy-start(bf16[1,384,2,128]{3,2,1,0:T(2,128)(2,1)} %stack_reshape.215) | copy-start | bytes 589828
  100.3 5.8 %copy-start.58 = (f32[16,8,128]{2,1,0:T(8,128)S(1)}, f32[16,8,128]{2,1,0:T(8,128)}, u32[]{:S(2)}) copy-start(f32[16,8,128]{2,1,0:T(8,128)} %compare_convert_fusion) | copy-start | bytes 196612
  101.8 5.7 %collective-permute-start.5 = (bf16[1,2,64,256]{3,2,1,0:T(8,128)(2,1)S(1)}, bf16[1,2,64,256]{3,2,1,0:T(8,128)(2,1)S(1)}, u32[]{:S(2)}, u32[]{:S(2)}) collective-permute-start(bf16[1,2,64,256]{3,2,1,0:T(8,128)(2,1)S(1)} %bitcast.291), channel_id=1, source_target_pairs={{2,0},{4,2},{6,4},{8,6},{10,8},{12,10},{14,12},{16,14},{18,16},{20... | collective-permute-start | bytes 196616 | tf_op jit(solution)/shard_map/ppermute | solution.py:17
  103.1 4.4 %collective-permute-start.4 = (bf16[1,2,64,256]{3,2,1,0:T(8,128)(2,1)S(1)}, bf16[1,2,64,256]{3,2,1,0:T(8,128)(2,1)S(1)}, u32[]{:S(2)}, u32[]{:S(2)}) collective-permute-start(bf16[1,2,64,256]{3,2,1,0:T(8,128)(2,1)S(1)} %bitcast.290), channel_id=1, source_target_pairs={{0,2},{2,4},{4,6},{6,8},{8,10},{10,12},{12,14},{14,16},{16,18},{18... | collective-permute-start | bytes 196616 | tf_op jit(solution)/shard_map/ppermute | solution.py:16
  107.6 6.7 %collective-permute-start.6 = (bf16[5,1,64,256]{3,2,1,0:T(8,128)(2,1)S(1)}, bf16[5,1,64,256]{3,2,1,0:T(8,128)(2,1)S(1)}, u32[]{:S(2)}, u32[]{:S(2)}) collective-permute-start(bf16[5,1,64,256]{3,2,1,0:T(8,128)(2,1)S(1)} %get-tuple-element.78), channel_id=1, source_target_pairs={{0,1},{2,3},{4,5},{6,7},{8,9},{10,11},{12,13},{14,15},{16,17},{18,... | collective-permute-start | bytes 491528 | tf_op jit(solution)/shard_map/ppermute | solution.py:16
  109.8 7.7 %collective-permute-start.7 = (bf16[5,1,64,256]{3,2,1,0:T(8,128)(2,1)S(1)}, bf16[5,1,64,256]{3,2,1,0:T(8,128)(2,1)S(1)}, u32[]{:S(2)}, u32[]{:S(2)}) collective-permute-start(bf16[5,1,64,256]{3,2,1,0:T(8,128)(2,1)S(1)} %get-tuple-element.79), channel_id=1, source_target_pairs={{1,0},{3,2},{5,4},{7,6},{9,8},{11,10},{13,12},{15,14},{17,16},{19,... | collective-permute-start | bytes 491528 | tf_op jit(solution)/shard_map/ppermute | solution.py:17
  (48 other events, 98.5 us)
Sparse Core Ops, SparseCore 0:
  155.5 133.4 all-reduce.4
where the time goes:
time: 302 us; the launch traced here: 301 us
  waiting for transfers between devices  138 us (46%)
  local copies, waits for them, and re-layouts  110 us (36%)
  starting transfers between devices  18.5 us (6%)
  matrix products  16.3 us (5%)
  between operations  14.9 us (5%)
  other arithmetic  3.25 us (1%)
    psum x1, waiting for transfers between devices, shards(): lax.psum((grad_in, grad_local, grad_out), ('inline', 'chan'))  132 us
    another operation x63, local copies, waits for them, and re-layouts, tap_stack(): return jnp.stack(pieces)  67.9 us
    unnamed x177, local copies, waits for them, and re-layouts  33.8 us
    ppermute x4, starting transfers between devices, extended_2(): before = lax.ppermute(last, axis, up)  13.2 us
    dot_general x3, matrix products, shards(): jnp.einsum('tnki,tkio->nko', stacked, dense[9 * aa:9 * aa + 9], preferred...  6.5 us
  transfers between devices with their start and end apart: 9, of which 3 were waited for; matrix products, arithmetic and copies ran while one was open for 4% of the time, Pallas kernels for 0%

commit v1 on v0

v1 whole, which is shorter than its diff:
```python
import functools
import math

import jax
import jax.numpy as jnp
from jax import lax
from jax.experimental import pallas as pl
from jax.experimental.pallas import tpu as pltpu
from jax.sharding import PartitionSpec as P

GW = 8
BF = jnp.bfloat16
F32 = jnp.float32
MESH = pl.DeviceIdType.MESH
DIRS = [(di, dc) for di in (-1, 0, 1) for dc in (-1, 0, 1) if (di, dc) != (0, 0)]


def sigmoid(v):
    return jax.nn.sigmoid(v)


def dot_nn(a, b):
    return jnp.dot(a, b, preferred_element_type=F32)


def dot_nt(a, b):
    return lax.dot_general(a, b, (((1,), (1,)), ((), ())), preferred_element_type=F32)


def kernel(
    cfg,
    x_ref, win_ref, wg_ref, wout_ref, cot_ref,
    out_ref, ig_ref, gin_ref, ggr_ref, gout_ref,
    rx, ext, dfwd, dbwd, pre_s, back_s, gtap, part, recv1, recv2, fin,
    hs_sem, hr_sem, as_sem, ar_sem, bs_sem, br_sem, cs_sem, cr_sem,
):
    ni, nc, na_i, na_c = cfg
    na = na_i * na_c
    nb_c = nc // na_c
    nb = (ni // na_i) * nb_c
    rows, cross, depth, chans = x_ref.shape
    cells = rows * cross * depth
    i = lax.axis_index("inline")
    c = lax.axis_index("chan")
    ga = lax.rem(i, na_i) * na_c + lax.rem(c, na_c)
    gb = lax.div(i, na_i) * nb_c + lax.div(c, na_c)

    def peer_a(r):
        g = lax.rem(ga + r, na)
        return (
            lax.div(i, na_i) * na_i + lax.div(g, na_c),
            lax.div(c, na_c) * na_c + lax.rem(g, na_c),
        )

    def peer_b(r):
        g = lax.rem(gb + r, nb)
        return (
            lax.div(g, nb_c) * na_i + lax.rem(i, na_i),
            lax.rem(g, nb_c) * na_c + lax.rem(c, na_c),
        )

    def has(di, dc):
        ok = None
        for step, at, size in ((di, i, ni), (dc, c, nc)):
            if step:
                one = at < size - 1 if step > 0 else at > 0
                ok = one if ok is None else jnp.logical_and(ok, one)
        return ok

    def neighbour(di, dc):
        return (lax.rem(i + di + ni, ni), lax.rem(c + dc + nc, nc))

    for e in range(2):
        for p in (0, rows + 1):
            rx[e, p] = jnp.zeros((cross + 2, depth, chans), BF)
        for q in (0, cross + 1):
            rx[e, 1 : rows + 1, q] = jnp.zeros((rows, depth, chans), BF)

    barrier = pltpu.get_barrier_semaphore()
    count = jnp.int32(na - 1 + nb - 1)
    for d in DIRS:
        @pl.when(has(*d))
        def _():
            pl.semaphore_signal(barrier, inc=1, device_id=neighbour(*d), device_id_type=MESH)

        count = count + has(*d).astype(jnp.int32)
    for r in range(1, na):
        pl.semaphore_signal(barrier, inc=1, device_id=peer_a(r), device_id_type=MESH)
    for r in range(1, nb):
        pl.semaphore_signal(barrier, inc=1, device_id=peer_b(r), device_id_type=MESH)

    def halo(e, k):
        di, dc = DIRS[k]
        src_i = {1: rows, -1: 1, 0: pl.ds(1, rows)}[di]
        dst_i = {1: 0, -1: rows + 1, 0: pl.ds(1, rows)}[di]
        src_c = {1: cross, -1: 1, 0: pl.ds(1, cross)}[dc]
        dst_c = {1: 0, -1: cross + 1, 0: pl.ds(1, cross)}[dc]
        return pltpu.make_async_remote_copy(
            src_ref=rx.at[e, src_i, src_c],
            dst_ref=rx.at[e, dst_i, dst_c],
            send_sem=hs_sem.at[e, k],
            recv_sem=hr_sem.at[e, k],
            device_id=neighbour(di, dc),
            device_id_type=MESH,
        )

    def halo_start(e):
        for k, d in enumerate(DIRS):
            @pl.when(has(*d))
            def _():
                halo(e, k).start()

    def halo_wait(e):
        for k, d in enumerate(DIRS):
            @pl.when(has(-d[0], -d[1]))
            def _():
                halo(e, k).wait_recv()

    def halo_sent(e):
        for k, d in enumerate(DIRS):
            @pl.when(has(*d))
            def _():
                halo(e, k).wait_send()

    def shifted(e, p0, p1, q0, q1):
        n = (p1 - p0) * (q1 - q0) * depth
        v = rx[e, p0:p1, q0:q1].reshape(n, chans)
        f = v.astype(F32)
        at = lax.rem(lax.broadcasted_iota(jnp.int32, (n, chans), 0), depth)
        up = jnp.where(at == 0, 0.0, pltpu.roll(f, 1, 0)).astype(BF)
        down = jnp.where(at == depth - 1, 0.0, pltpu.roll(f, n - 1, 0)).astype(BF)
        shape = (p1 - p0, q1 - q0, depth, chans)
        for s, piece in enumerate((up, v, down)):
            ext[e, p0:p1, q0:q1, :, s * chans : (s + 1) * chans] = piece.reshape(shape)

    def shifted_inner(e):
        shifted(e, 1, rows + 1, 1, cross + 1)

    def shifted_edges(e):
        shifted(e, 0, 1, 0, cross + 2)
        shifted(e, rows + 1, rows + 2, 0, cross + 2)
        shifted(e, 1, rows + 1, 0, 1)
        shifted(e, 1, rows + 1, cross + 1, cross + 2)

    def window(e, a):
        return jnp.concatenate(
            [ext[e, a : a + rows, b : b + cross].reshape(cells, 3 * chans) for b in range(3)],
            axis=1,
        )

    def scatter(q, r):
        return pltpu.make_async_remote_copy(
            src_ref=part.at[q, lax.rem(ga + r, na)],
            dst_ref=recv1.at[q, r],
            send_sem=as_sem.at[q, r],
            recv_sem=ar_sem.at[q, r],
            device_id=peer_a(r),
            device_id_type=MESH,
        )

    def spread(q, r, slot):
        return pltpu.make_async_remote_copy(
            src_ref=recv2.at[q, gb],
            dst_ref=recv2.at[q, slot],
            send_sem=bs_sem.at[q, r],
            recv_sem=br_sem.at[q, r],
            device_id=peer_b(r),
            device_id_type=MESH,
        )

    def gather(q, r, slot):
        return pltpu.make_async_remote_copy(
            src_ref=fin.at[q, ga],
            dst_ref=fin.at[q, slot],
            send_sem=cs_sem.at[q, r],
            recv_sem=cr_sem.at[q, r],
            device_id=peer_a(r),
            device_id_type=MESH,
        )

    def sum_start(q, value):
        part[q] = value.astype(BF).reshape(na, chans // na, chans)
        for r in range(1, na):
            scatter(q, r).start()

    def sum_spread(q):
        for r in range(1, na):
            scatter(q, r).wait_recv()
        total = part[q, ga].astype(F32)
        for r in range(1, na):
            total = total + recv1[q, r].astype(F32)
        recv2[q, gb] = total.astype(BF)
        for r in range(1, nb):
            spread(q, r, gb).start()

    def sum_gather(q):
        for r in range(1, nb):
            spread(q, r, lax.rem(gb + nb - r, nb)).wait_recv()
        total = recv2[q, 0].astype(F32)
        for s in range(1, nb):
            total = total + recv2[q, s].astype(F32)
        fin[q, ga] = total.astype(BF)
        for r in range(1, na):
            gather(q, r, ga).start()

    def sum_done(q):
        for r in range(1, na):
            gather(q, r, lax.rem(ga + na - r, na)).wait_recv()
        return fin[q].astype(F32).reshape(chans, chans)

    def sum_sent(q):
        for r in range(1, na):
            scatter(q, r).wait_send()
        for r in range(1, nb):
            spread(q, r, gb).wait_send()
        for r in range(1, na):
            gather(q, r, ga).wait_send()

    full = (rows, cross, depth, chans)
    x = x_ref[...].reshape(cells, chans)
    pre = dot_nn(x, win_ref[...])
    pre_s[...] = pre
    rx[0, 1 : rows + 1, 1 : cross + 1] = (pre * sigmoid(pre)).astype(BF).reshape(full)
    pl.semaphore_wait(barrier, count)
    halo_start(0)

    same = lax.div(lax.broadcasted_iota(jnp.int32, (chans, chans), 0), GW) == lax.div(
        lax.broadcasted_iota(jnp.int32, (chans, chans), 1), GW
    )

    def build(a, carry):
        for u in range(9):
            w = wg_ref[a * 9 + u].astype(F32)
            tiled = jnp.broadcast_to(w[None], (chans // GW, GW, chans)).reshape(chans, chans)
            dense = jnp.where(same, tiled, 0.0).astype(BF)
            dfwd[a, u * chans : (u + 1) * chans, :] = dense
            dbwd[2 - a, :, (8 - u) * chans : (9 - u) * chans] = dense
        return carry

    lax.fori_loop(0, 3, build, 0)
    shifted_inner(0)
    back_s[...] = dot_nt(cot_ref[...].reshape(cells, chans), wout_ref[...])
    halo_wait(0)
    shifted_edges(0)

    conv = dot_nn(window(0, 0), dfwd[0])
    for a in (1, 2):
        conv = conv + dot_nn(window(0, a), dfwd[a])
    sig = sigmoid(conv)
    second = (conv * sig).astype(BF)
    grad_conv = (back_s[...] * (sig * (1.0 + conv * (1.0 - sig)))).astype(BF)
    rx[1, 1 : rows + 1, 1 : cross + 1] = grad_conv.reshape(full)
    halo_start(1)

    sum_start(0, dot_nn(second.T, cot_ref[...].reshape(cells, chans)))
    mixed = dot_nn(second, wout_ref[...])
    out_ref[...] = (x_ref[...].reshape(cells, chans).astype(F32) + mixed).astype(BF).reshape(full)
    shifted_inner(1)

    gtap[...] = jnp.zeros(gtap.shape, F32)

    def taps(b, carry):
        for s in range(3):
            block = ext[0, :, pl.ds(b, cross), :, s * chans : (s + 1) * chans]
            turned = block.reshape((rows + 2) * cross * depth, chans).T
            for a in range(3):
                begin = a * cross * depth
                g = dot_nn(
                    turned[:, begin : begin + cells],
                    rx[1, 1 : rows + 1, 1 : cross + 1].reshape(cells, chans),
                )
                g = jnp.where(same, g, 0.0).reshape(chans // GW, GW, chans)
                gtap[9 * a + 3 * b + s] = jnp.sum(g, axis=0)
        return carry

    lax.fori_loop(0, 3, taps, 0)
    sum_spread(0)
    sum_start(1, gtap[...].reshape(chans, chans))

    halo_wait(1)
    shifted_edges(1)
    back = dot_nt(window(1, 0), dbwd[0])
    for a in (1, 2):
        back = back + dot_nt(window(1, a), dbwd[a])
    sum_gather(0)
    sum_spread(1)
    pre = pre_s[...]
    sig = sigmoid(pre)
    mixed = (back * (sig * (1.0 + pre * (1.0 - sig)))).astype(BF)
    sum_start(2, dot_nn(x_ref[...].reshape(cells, chans).T, mixed))
    back_in = dot_nt(mixed, win_ref[...])
    cot32 = cot_ref[...].reshape(cells, chans).astype(F32)
    ig_ref[...] = (cot32 + back_in).astype(BF).reshape(full)
    sum_gather(1)
    sum_spread(2)
    gout_ref[...] = sum_done(0)
    sum_gather(2)
    ggr_ref[...] = sum_done(1)[: 27 * GW].reshape(27, GW, chans)
    gin_ref[...] = sum_done(2)
    for e in range(2):
        halo_sent(e)
    for q in range(3):
        sum_sent(q)


def shards(cfg, inputs, w_in, w_group, w_out, cotangent):
    ni, nc, na_i, na_c = cfg
    na = na_i * na_c
    nb = ni * nc // na
    rows, cross, depth, chans = inputs.shape
    cells = rows * cross * depth
    slab = (chans // na, chans)
    vmem = pl.BlockSpec(memory_space=pltpu.VMEM)
    dma = pltpu.SemaphoreType.DMA
    return pl.pallas_call(
        functools.partial(kernel, cfg),
        out_shape=(
            jax.ShapeDtypeStruct(inputs.shape, BF),
            jax.ShapeDtypeStruct(inputs.shape, BF),
            jax.ShapeDtypeStruct((chans, chans), F32),
            jax.ShapeDtypeStruct(w_group.shape, F32),
            jax.ShapeDtypeStruct((chans, chans), F32),
        ),
        in_specs=[vmem] * 5,
        out_specs=(vmem,) * 5,
        scratch_shapes=[
            pltpu.VMEM((2, rows + 2, cross + 2, depth, chans), BF),
            pltpu.VMEM((2, rows + 2, cross + 2, depth, 3 * chans), BF),
            pltpu.VMEM((3, 9 * chans, chans), BF),
            pltpu.VMEM((3, chans, 9 * chans), BF),
            pltpu.VMEM((cells, chans), F32),
            pltpu.VMEM((cells, chans), F32),
            pltpu.VMEM((chans // GW, GW, chans), F32),
            pltpu.VMEM((3, na) + slab, BF),
            pltpu.VMEM((3, na) + slab, BF),
            pltpu.VMEM((3, nb) + slab, BF),
            pltpu.VMEM((3, na) + slab, BF),
            dma((2, 8)),
            dma((2, 8)),
            dma((3, na)),
            dma((3, na)),
            dma((3, nb)),
            dma((3, nb)),
            dma((3, na)),
            dma((3, na)),
        ],
        compiler_params=pltpu.CompilerParams(
            collective_id=0, has_side_effects=True, vmem_limit_bytes=48 * 1024 * 1024
        ),
    )(inputs, w_in, w_group, w_out, cotangent)


def solution(mesh):
    ni, nc = mesh.shape["inline"], mesh.shape["chan"]
    cfg = (ni, nc, math.gcd(ni, 4), math.gcd(nc, 2))
    field = P("inline", "chan", None, None)
    return jax.shard_map(
        functools.partial(shards, cfg),
        mesh=mesh,
        in_specs=(field, P(), P(), P(), field),
        out_specs=(field, field, P(), P(), P()),
        check_vma=False,
    )
```

time: 302 us -> 45.1 us (0.15)
  waiting for transfers between devices: 138 us -> 0 us
  local copies, waits for them, and re-layouts: 110 us -> 7.99 us
  Pallas kernels: 0 us -> 36.2 us
  starting transfers between devices: 18.5 us -> 0 us
  matrix products: 16.3 us -> 0 us
  between operations: 14.9 us -> 0.66 us
  other arithmetic: 3.25 us -> 0 us
    psum x1 -> x0, waiting for transfers between devices: 132 us -> none  [shards(): lax.psum((grad_in, grad_local, grad_out), ('inline', 'chan'))]
    another operation x65 -> x0, local copies, waits for them, and re-layouts: 72.1 us -> none  [the longest x63 67.9 us: tap_stack(): return jnp.stack(pieces)]
    pallas_call x0 -> x1, Pallas kernels: none -> 36.2 us  [shards(): pl.pallas_call(functools.partial(kernel, cfg), out_shape=(jax.ShapeDtypeS...]
    unnamed x177 -> x15, local copies, waits for them, and re-layouts: 33.8 us -> 7.99 us
    ppermute x8 -> x0, starting transfers between devices: 18.5 us -> none  [the longest x4 13.2 us: extended_2(): before = lax.ppermute(last, axis, up)]
    dot_general x12 -> x0, matrix products: 14.5 us -> none  [the longest x3 6.5 us: shards(): jnp.einsum('tnki,tkio->nko', stacked, dense[9 * aa:9 * aa + 9], preferred...]
    ppermute x8 -> x0, waiting for transfers between devices: 5.79 us -> none  [the longest x4 5.78 us: extended_2(): after = lax.ppermute(leading, axis, down)]
    slice x9 -> x0, local copies, waits for them, and re-layouts: 3.42 us -> none  [the longest x5 3.35 us: tap_stack(): padded[begin_a:begin_a + rows, begin_b:begin_b + cross, begin_c:begin_c +...]
  transfers between devices with their start and end apart: 9 -> 0, of which waited for: 3 -> 0; matrix products, arithmetic and copies ran while one was open for 4% -> 0% of each run, Pallas kernels for 0% -> 0%
where the time goes in v1:
time: 45.1 us; the launch traced here: 44.8 us
  Pallas kernels  36.2 us (80%)
  local copies, waits for them, and re-layouts  7.99 us (18%)
  between operations  0.66 us (1%)
    pallas_call x1, Pallas kernels, shards(): pl.pallas_call(functools.partial(kernel, cfg), out_shape=(jax.ShapeDtypeS...  36.2 us
    unnamed x15, local copies, waits for them, and re-layouts  7.99 us

profile of v1, /device:TPU:0, one launch (start us, length us, event | category | flops | bytes accessed | tf_op | source)
XLA Modules:
  0.0 44.8 jit_solution(11408484542417447594)
XLA Ops:
  0.6 0.0 copy-start
  0.6 0.9 %copy-done = bf16[3,2,64,256]{3,2,1,0:T(8,128)(2,1)S(1)} copy-done((bf16[3,2,64,256]{3,2,1,0:T(8,128)(2,1)S(1)}, bf16[3,2,64,256]{3,2,1,0:T(8,128)(2,1)}, u32[]{:S(2)}) %copy-start) | copy-done | bytes 196632
  1.6 0.0 copy-start.1
  1.6 0.9 %copy-done.1 = bf16[3,2,64,256]{3,2,1,0:T(8,128)(2,1)S(1)} copy-done((bf16[3,2,64,256]{3,2,1,0:T(8,128)(2,1)S(1)}, bf16[3,2,64,256]{3,2,1,0:T(8,128)(2,1)}, u32[]{:S(2)}) %copy-start.1) | copy-done | bytes 196632
  2.5 0.0 copy-start.2
  2.5 0.9 %copy-done.2 = bf16[256,256]{1,0:T(8,128)(2,1)S(1)} copy-done((bf16[256,256]{1,0:T(8,128)(2,1)S(1)}, bf16[256,256]{1,0:T(8,128)(2,1)}, u32[]{:S(2)}) %copy-start.2) | copy-done | bytes 131096
  3.4 0.0 copy-start.3
  3.4 0.9 %copy-done.3 = bf16[256,256]{1,0:T(8,128)(2,1)S(1)} copy-done((bf16[256,256]{1,0:T(8,128)(2,1)S(1)}, bf16[256,256]{1,0:T(8,128)(2,1)}, u32[]{:S(2)}) %copy-start.3) | copy-done | bytes 131096
  4.3 0.0 copy-start.4
  4.3 0.9 %copy-done.4 = bf16[27,8,256]{2,1,0:T(8,128)(2,1)S(1)} copy-done((bf16[27,8,256]{2,1,0:T(8,128)(2,1)S(1)}, bf16[27,8,256]{2,1,0:T(8,128)(2,1)}, u32[]{:S(2)}) %copy-start.4) | copy-done | bytes 110616
  5.2 36.2 %shard_map.92 = (bf16[3,2,64,256]{3,2,1,0:T(8,128)(2,1)S(1)}, bf16[3,2,64,256]{3,2,1,0:T(8,128)(2,1)S(1)}, f32[256,256]{1,0:T(8,128)S(1)}, f32[27,8,256]{2,1,0:T(8,128)S(1)}, f32[256,256]{1,0:T(8,128)S(1)}) custom-call(bf16[3,2,64,256]{3,2,1,0:T(8,128)(2,1)S(1)} %copy-done, bf16[256,256]{1,0:T(8,128)(2,1)S(1)} %copy-done.2, ...), custom_call_target="tpu_custom_call" | custom-call | tf_op jit(solution)/shard_map/pallas_call | solution.py:315
  41.4 0.7 %copy.15 = bf16[3,2,64,256]{3,2,1,0:T(8,128)(2,1)} copy(bf16[3,2,64,256]{3,2,1,0:T(8,128)(2,1)S(1)} %get-tuple-element.10) | data formatting | bytes 393216
  42.1 0.7 %copy.16 = bf16[3,2,64,256]{3,2,1,0:T(8,128)(2,1)} copy(bf16[3,2,64,256]{3,2,1,0:T(8,128)(2,1)S(1)} %get-tuple-element.11) | data formatting | bytes 393216
  42.7 0.7 %copy.17 = f32[256,256]{1,0:T(8,128)} copy(f32[256,256]{1,0:T(8,128)S(1)} %get-tuple-element.12) | data formatting | bytes 524288
  43.4 0.7 %copy.18 = f32[27,8,256]{2,1,0:T(8,128)} copy(f32[27,8,256]{2,1,0:T(8,128)S(1)} %get-tuple-element.13) | data formatting | bytes 442368
  44.1 0.7 %copy.19 = f32[256,256]{1,0:T(8,128)} copy(f32[256,256]{1,0:T(8,128)S(1)} %get-tuple-element.14) | data formatting | bytes 524288
Async XLA Ops:
  0.6 0.9 %copy-start = (bf16[3,2,64,256]{3,2,1,0:T(8,128)(2,1)S(1)}, bf16[3,2,64,256]{3,2,1,0:T(8,128)(2,1)}, u32[]{:S(2)}) copy-start(bf16[3,2,64,256]{3,2,1,0:T(8,128)(2,1)} %x_ref.1) | copy-start | bytes 589828
  1.6 0.9 %copy-start.1 = (bf16[3,2,64,256]{3,2,1,0:T(8,128)(2,1)S(1)}, bf16[3,2,64,256]{3,2,1,0:T(8,128)(2,1)}, u32[]{:S(2)}) copy-start(bf16[3,2,64,256]{3,2,1,0:T(8,128)(2,1)} %cot_ref.1) | copy-start | bytes 589828
  2.5 0.9 %copy-start.2 = (bf16[256,256]{1,0:T(8,128)(2,1)S(1)}, bf16[256,256]{1,0:T(8,128)(2,1)}, u32[]{:S(2)}) copy-start(bf16[256,256]{1,0:T(8,128)(2,1)} %win_ref.1) | copy-start | bytes 393220
  3.4 0.9 %copy-start.3 = (bf16[256,256]{1,0:T(8,128)(2,1)S(1)}, bf16[256,256]{1,0:T(8,128)(2,1)}, u32[]{:S(2)}) copy-start(bf16[256,256]{1,0:T(8,128)(2,1)} %wout_ref.1) | copy-start | bytes 393220
  4.3 0.9 %copy-start.4 = (bf16[27,8,256]{2,1,0:T(8,128)(2,1)S(1)}, bf16[27,8,256]{2,1,0:T(8,128)(2,1)}, u32[]{:S(2)}) copy-start(bf16[27,8,256]{2,1,0:T(8,128)(2,1)} %wg_ref.1) | copy-start | bytes 331780

commit v2 on v1

--- a/solution.py
+++ b/solution.py
@@ -29,11 +29,27 @@
 
 def kernel(
     cfg,
-    x_ref, win_ref, wg_ref, wout_ref, cot_ref,
+    x_hbm, win_hbm, wg_hbm, wout_hbm, cot_hbm,
     out_ref, ig_ref, gin_ref, ggr_ref, gout_ref,
-    rx, ext, dfwd, dbwd, pre_s, back_s, gtap, part, recv1, recv2, fin,
-    hs_sem, hr_sem, as_sem, ar_sem, bs_sem, br_sem, cs_sem, cr_sem,
+    x_ref, win_ref, wg_ref, wout_ref, cot_ref, in_sem,
+    rx, ext, dfwd, dbwd, pre_s, back_s, gtap, *sums,
 ):
+    part, recv1, recv2, fin = zip(sums[0:4], sums[4:8])
+    hs_sem, hr_sem, as_sem, ar_sem, bs_sem, br_sem, cs_sem, cr_sem = sums[8:]
+    fetch = [
+        pltpu.make_async_copy(src, dst, in_sem.at[k])
+        for k, (src, dst) in enumerate(
+            (
+                (x_hbm, x_ref),
+                (win_hbm, win_ref),
+                (wg_hbm, wg_ref),
+                (wout_hbm, wout_ref),
+                (cot_hbm, cot_ref),
+            )
+        )
+    ]
+    for one in fetch:
+        one.start()
     ni, nc, na_i, na_c = cfg
     na = na_i * na_c
     nb_c = nc // na_c
@@ -150,8 +166,8 @@
 
     def scatter(q, r):
         return pltpu.make_async_remote_copy(
-            src_ref=part.at[q, lax.rem(ga + r, na)],
-            dst_ref=recv1.at[q, r],
+            src_ref=part[q].at[lax.rem(ga + r, na)],
+            dst_ref=recv1[q].at[r],
             send_sem=as_sem.at[q, r],
             recv_sem=ar_sem.at[q, r],
             device_id=peer_a(r),
@@ -160,8 +176,8 @@
 
     def spread(q, r, slot):
         return pltpu.make_async_remote_copy(
-            src_ref=recv2.at[q, gb],
-            dst_ref=recv2.at[q, slot],
+            src_ref=recv2[q].at[gb],
+            dst_ref=recv2[q].at[slot],
             send_sem=bs_sem.at[q, r],
             recv_sem=br_sem.at[q, r],
             device_id=peer_b(r),
@@ -170,43 +186,49 @@
 
     def gather(q, r, slot):
         return pltpu.make_async_remote_copy(
-            src_ref=fin.at[q, ga],
-            dst_ref=fin.at[q, slot],
+            src_ref=fin[q].at[ga],
+            dst_ref=fin[q].at[slot],
             send_sem=cs_sem.at[q, r],
             recv_sem=cr_sem.at[q, r],
             device_id=peer_a(r),
             device_id_type=MESH,
         )
 
-    def sum_start(q, value):
-        part[q] = value.astype(BF).reshape(na, chans // na, chans)
+    def sum_start(q, *values):
+        for k, value in enumerate(values):
+            step = chans // na
+            part[q][:, k * step : (k + 1) * step] = value.astype(BF).reshape(na, step, chans)
         for r in range(1, na):
             scatter(q, r).start()
 
     def sum_spread(q):
         for r in range(1, na):
             scatter(q, r).wait_recv()
-        total = part[q, ga].astype(F32)
-        for r in range(1, na):
-            total = total + recv1[q, r].astype(F32)
-        recv2[q, gb] = total.astype(BF)
+        total = part[q][ga].astype(F32)
+        for r in range(1, na):
+            total = total + recv1[q][r].astype(F32)
+        recv2[q][gb] = total.astype(BF)
         for r in range(1, nb):
             spread(q, r, gb).start()
 
     def sum_gather(q):
         for r in range(1, nb):
             spread(q, r, lax.rem(gb + nb - r, nb)).wait_recv()
-        total = recv2[q, 0].astype(F32)
+        total = recv2[q][0].astype(F32)
         for s in range(1, nb):
-            total = total + recv2[q, s].astype(F32)
-        fin[q, ga] = total.astype(BF)
+            total = total + recv2[q][s].astype(F32)
+        fin[q][ga] = total.astype(BF)
         for r in range(1, na):
             gather(q, r, ga).start()
 
     def sum_done(q):
         for r in range(1, na):
             gather(q, r, lax.rem(ga + na - r, na)).wait_recv()
-        return fin[q].astype(F32).reshape(chans, chans)
+        step = chans // na
+        return [
+            fin[q][:, k * step : (k + 1) * step].astype(F32).reshape(chans, chans)
+            for k in range(fin[q].shape[1] // step)
+        ]
 
     def sum_sent(q):
         for r in range(1, na):
@@ -217,6 +239,8 @@
             gather(q, r, ga).wait_send()
 
     full = (rows, cross, depth, chans)
+    fetch[0].wait()
+    fetch[1].wait()
     x = x_ref[...].reshape(cells, chans)
     pre = dot_nn(x, win_ref[...])
     pre_s[...] = pre
@@ -237,8 +261,11 @@
             dbwd[2 - a, :, (8 - u) * chans : (9 - u) * chans] = dense
         return carry
 
+    fetch[2].wait()
     lax.fori_loop(0, 3, build, 0)
     shifted_inner(0)
+    fetch[3].wait()
+    fetch[4].wait()
     back_s[...] = dot_nt(cot_ref[...].reshape(cells, chans), wout_ref[...])
     halo_wait(0)
     shifted_edges(0)
@@ -252,7 +279,8 @@
     rx[1, 1 : rows + 1, 1 : cross + 1] = grad_conv.reshape(full)
     halo_start(1)
 
-    sum_start(0, dot_nn(second.T, cot_ref[...].reshape(cells, chans)))
+    grad_out = dot_nn(second.T, cot_ref[...].reshape(cells, chans))
+    back_s[0:chans] = grad_out
     mixed = dot_nn(second, wout_ref[...])
     out_ref[...] = (x_ref[...].reshape(cells, chans).astype(F32) + mixed).astype(BF).reshape(full)
     shifted_inner(1)
@@ -274,33 +302,40 @@
         return carry
 
     lax.fori_loop(0, 3, taps, 0)
-    sum_spread(0)
-    sum_start(1, gtap[...].reshape(chans, chans))
+    sum_start(0, back_s[0:chans], gtap[...].reshape(chans, chans))
 
     halo_wait(1)
     shifted_edges(1)
     back = dot_nt(window(1, 0), dbwd[0])
     for a in (1, 2):
         back = back + dot_nt(window(1, a), dbwd[a])
-    sum_gather(0)
-    sum_spread(1)
+    sum_spread(0)
     pre = pre_s[...]
     sig = sigmoid(pre)
     mixed = (back * (sig * (1.0 + pre * (1.0 - sig)))).astype(BF)
-    sum_start(2, dot_nn(x_ref[...].reshape(cells, chans).T, mixed))
+    sum_start(1, dot_nn(x_ref[...].reshape(cells, chans).T, mixed))
     back_in = dot_nt(mixed, win_ref[...])
     cot32 = cot_ref[...].reshape(cells, chans).astype(F32)
     ig_ref[...] = (cot32 + back_in).astype(BF).reshape(full)
+    sum_gather(0)
+    sum_spread(1)
+    gout_ref[...], group = sum_done(0)
+    ggr_ref[...] = group[: 27 * GW].reshape(27, GW, chans)
     sum_gather(1)
-    sum_spread(2)
-    gout_ref[...] = sum_done(0)
-    sum_gather(2)
-    ggr_ref[...] = sum_done(1)[: 27 * GW].reshape(27, GW, chans)
-    gin_ref[...] = sum_done(2)
+    (gin_ref[...],) = sum_done(1)
     for e in range(2):
         halo_sent(e)
-    for q in range(3):
+    for q in range(2):
         sum_sent(q)
+
+
+def store(*refs):
+    sem = refs[-1]
+    copies = [pltpu.make_async_copy(refs[k], refs[5 + k], sem.at[k]) for k in range(5)]
+    for one in copies:
+        one.start()
+    for one in copies:
+        one.wait()
 
 
 def shards(cfg, inputs, w_in, w_group, w_out, cotangent):
@@ -312,7 +347,7 @@
     slab = (chans // na, chans)
     vmem = pl.BlockSpec(memory_space=pltpu.VMEM)
     dma = pltpu.SemaphoreType.DMA
-    return pl.pallas_call(
+    results = pl.pallas_call(
         functools.partial(kernel, cfg),
         out_shape=(
             jax.ShapeDtypeStruct(inputs.shape, BF),
@@ -321,9 +356,11 @@
             jax.ShapeDtypeStruct(w_group.shape, F32),
             jax.ShapeDtypeStruct((chans, chans), F32),
         ),
-        in_specs=[vmem] * 5,
+        in_specs=[pl.BlockSpec(memory_space=pltpu.HBM)] * 5,
         out_specs=(vmem,) * 5,
         scratch_shapes=[
+            *(pltpu.VMEM(one.shape, BF) for one in (inputs, w_in, w_group, w_out, cotangent)),
+            dma((5,)),
             pltpu.VMEM((2, rows + 2, cross + 2, depth, chans), BF),
             pltpu.VMEM((2, rows + 2, cross + 2, depth, 3 * chans), BF),
             pltpu.VMEM((3, 9 * chans, chans), BF),
@@ -331,23 +368,31 @@
             pltpu.VMEM((cells, chans), F32),
             pltpu.VMEM((cells, chans), F32),
             pltpu.VMEM((chans // GW, GW, chans), F32),
-            pltpu.VMEM((3, na) + slab, BF),
-            pltpu.VMEM((3, na) + slab, BF),
-            pltpu.VMEM((3, nb) + slab, BF),
-            pltpu.VMEM((3, na) + slab, BF),
+            *(
+                pltpu.VMEM((count, depth_of * slab[0], chans), BF)
+                for depth_of in (2, 1)
+                for count in (na, na, nb, na)
+            ),
             dma((2, 8)),
             dma((2, 8)),
-            dma((3, na)),
-            dma((3, na)),
-            dma((3, nb)),
-            dma((3, nb)),
-            dma((3, na)),
-            dma((3, na)),
+            dma((2, na)),
+            dma((2, na)),
+            dma((2, nb)),
+            dma((2, nb)),
+            dma((2, na)),
+            dma((2, na)),
         ],
         compiler_params=pltpu.CompilerParams(
-            collective_id=0, has_side_effects=True, vmem_limit_bytes=48 * 1024 * 1024
+            collective_id=0, has_side_effects=True, vmem_limit_bytes=64137 * 1024
         ),
     )(inputs, w_in, w_group, w_out, cotangent)
+    return pl.pallas_call(
+        store,
+        out_shape=tuple(jax.ShapeDtypeStruct(one.shape, one.dtype) for one in results),
+        in_specs=[vmem] * 5,
+        out_specs=(pl.BlockSpec(memory_space=pltpu.HBM),) * 5,
+        scratch_shapes=[dma((5,))],
+    )(*results)
 
 
 def solution(mesh):

time: 45.1 us -> 38.5 us (0.85)
  local copies, waits for them, and re-layouts: 7.99 us -> 0 us
  Pallas kernels: 36.2 us -> 37.7 us
    unnamed x15 -> x0, local copies, waits for them, and re-layouts: 7.99 us -> none
    pallas_call x0 -> x1, Pallas kernels: none -> 2.37 us  [shards(): pl.pallas_call(store, out_shape=tuple((jax.ShapeDtypeStruct(one.shape, on...]
    pallas_call x1, Pallas kernels: 36.2 us -> 35.4 us  [shards(): pl.pallas_call(functools.partial(kernel, cfg), out_shape=(jax.ShapeDtypeS...]
where the time goes in v2:
time: 38.5 us; the launch traced here: 38.4 us
  Pallas kernels  37.7 us (98%)
  between operations  0.64 us (2%)
    pallas_call x1, Pallas kernels, shards(): pl.pallas_call(functools.partial(kernel, cfg), out_shape=(jax.ShapeDtypeS...  35.4 us
    pallas_call x1, Pallas kernels, shards(): pl.pallas_call(store, out_shape=tuple((jax.ShapeDtypeStruct(one.shape, on...  2.37 us

profile of v2, /device:TPU:0, one launch (start us, length us, event | category | flops | bytes accessed | tf_op | source)
XLA Modules:
  0.0 38.4 jit_solution(3960076958693514918)
XLA Ops:
  0.6 35.4 %shard_map.92 = (bf16[3,2,64,256]{3,2,1,0:T(8,128)(2,1)}, bf16[3,2,64,256]{3,2,1,0:T(8,128)(2,1)}, f32[256,256]{1,0:T(8,128)}, f32[27,8,256]{2,1,0:T(8,128)}, f32[256,256]{1,0:T(8,128)}) custom-call(bf16[3,2,64,256]{3,2,1,0:T(8,128)(2,1)} %x_hbm.1, bf16[256,256]{1,0:T(8,128)(2,1)} %win_hbm.1, bf16[27,8,256]{2,1,0:T(8,128)(2,1)} %wg_hbm.1, ...), custom_call_target="tpu_custom_call" | custom-call | tf_op jit(solution)/shard_map/pallas_call | solution.py:350
  36.0 2.4 %shard_map.93 = (bf16[3,2,64,256]{3,2,1,0:T(8,128)(2,1)}, bf16[3,2,64,256]{3,2,1,0:T(8,128)(2,1)}, f32[256,256]{1,0:T(8,128)}, f32[27,8,256]{2,1,0:T(8,128)}, f32[256,256]{1,0:T(8,128)}) custom-call(bf16[3,2,64,256]{3,2,1,0:T(8,128)(2,1)} %get-tuple-element.10.refs_0_, bf16[3,2,64,256]{3,2,1,0:T(8,128)(2,1)} %get-tuple-element.11.refs_1_, ...), custom_call_target="tpu_custom_call" | custom-call | tf_op jit(solution)/shard_map/pallas_call | solution.py:389

commit v3 on v2

--- a/solution.py
+++ b/solution.py
@@ -30,7 +30,8 @@
 def kernel(
     cfg,
     x_hbm, win_hbm, wg_hbm, wout_hbm, cot_hbm,
-    out_ref, ig_ref, gin_ref, ggr_ref, gout_ref,
+    out_hbm, ig_hbm, gin_hbm, ggr_hbm, gout_hbm,
+    out_ref, ig_ref, gin_ref, ggr_ref, gout_ref, out_sem, turned_x,
     x_ref, win_ref, wg_ref, wout_ref, cot_ref, in_sem,
     rx, ext, dfwd, dbwd, pre_s, back_s, gtap, *sums,
 ):
@@ -48,6 +49,18 @@
             )
         )
     ]
+    keep = [
+        pltpu.make_async_copy(src, dst, out_sem.at[k])
+        for k, (src, dst) in enumerate(
+            (
+                (out_ref, out_hbm),
+                (ig_ref, ig_hbm),
+                (gin_ref, gin_hbm),
+                (ggr_ref, ggr_hbm),
+                (gout_ref, gout_hbm),
+            )
+        )
+    ]
     for one in fetch:
         one.start()
     ni, nc, na_i, na_c = cfg
@@ -267,6 +280,7 @@
     fetch[3].wait()
     fetch[4].wait()
     back_s[...] = dot_nt(cot_ref[...].reshape(cells, chans), wout_ref[...])
+    turned_x[...] = x_ref[...].reshape(cells, chans).T
     halo_wait(0)
     shifted_edges(0)
 
@@ -284,6 +298,7 @@
     mixed = dot_nn(second, wout_ref[...])
     out_ref[...] = (x_ref[...].reshape(cells, chans).astype(F32) + mixed).astype(BF).reshape(full)
     shifted_inner(1)
+    keep[0].start()
 
     gtap[...] = jnp.zeros(gtap.shape, F32)
 
@@ -309,32 +324,42 @@
     back = dot_nt(window(1, 0), dbwd[0])
     for a in (1, 2):
         back = back + dot_nt(window(1, a), dbwd[a])
-    sum_spread(0)
     pre = pre_s[...]
     sig = sigmoid(pre)
     mixed = (back * (sig * (1.0 + pre * (1.0 - sig)))).astype(BF)
-    sum_start(1, dot_nn(x_ref[...].reshape(cells, chans).T, mixed))
+    sum_start(1, dot_nn(turned_x[...], mixed))
     back_in = dot_nt(mixed, win_ref[...])
     cot32 = cot_ref[...].reshape(cells, chans).astype(F32)
     ig_ref[...] = (cot32 + back_in).astype(BF).reshape(full)
+    sum_spread(0)
+    keep[1].start()
+    sum_spread(1)
     sum_gather(0)
-    sum_spread(1)
+    sum_gather(1)
     gout_ref[...], group = sum_done(0)
     ggr_ref[...] = group[: 27 * GW].reshape(27, GW, chans)
-    sum_gather(1)
+    keep[3].start()
+    keep[4].start()
     (gin_ref[...],) = sum_done(1)
+    keep[2].start()
     for e in range(2):
         halo_sent(e)
     for q in range(2):
         sum_sent(q)
+    for one in keep:
+        one.wait()
 
 
 def store(*refs):
-    sem = refs[-1]
-    copies = [pltpu.make_async_copy(refs[k], refs[5 + k], sem.at[k]) for k in range(5)]
-    for one in copies:
+    before, after = refs[-2:]
+    loads = [pltpu.make_async_copy(refs[k], refs[10 + k], before.at[k]) for k in range(5)]
+    stores = [pltpu.make_async_copy(refs[10 + k], refs[5 + k], after.at[k]) for k in range(5)]
+    for one in loads:
         one.start()
-    for one in copies:
+    for load, one in zip(loads, stores):
+        load.wait()
+        one.start()
+    for one in stores:
         one.wait()
 
 
@@ -345,7 +370,9 @@
     rows, cross, depth, chans = inputs.shape
     cells = rows * cross * depth
     slab = (chans // na, chans)
-    vmem = pl.BlockSpec(memory_space=pltpu.VMEM)
+    hbm = pl.BlockSpec(memory_space=pltpu.HBM)
+    whole = ((inputs, BF), (inputs, BF), (w_in, F32), (w_group, F32), (w_out, F32))
+    staged = [pltpu.VMEM(one.shape, kind) for one, kind in whole]
     dma = pltpu.SemaphoreType.DMA
     results = pl.pallas_call(
         functools.partial(kernel, cfg),
@@ -357,8 +384,11 @@
             jax.ShapeDtypeStruct((chans, chans), F32),
         ),
         in_specs=[pl.BlockSpec(memory_space=pltpu.HBM)] * 5,
-        out_specs=(vmem,) * 5,
+        out_specs=(hbm,) * 5,
         scratch_shapes=[
+            *staged,
+            dma((5,)),
+            pltpu.VMEM((chans, cells), BF),
             *(pltpu.VMEM(one.shape, BF) for one in (inputs, w_in, w_group, w_out, cotangent)),
             dma((5,)),
             pltpu.VMEM((2, rows + 2, cross + 2, depth, chans), BF),
@@ -389,9 +419,10 @@
     return pl.pallas_call(
         store,
         out_shape=tuple(jax.ShapeDtypeStruct(one.shape, one.dtype) for one in results),
-        in_specs=[vmem] * 5,
+        in_specs=[hbm] * 5,
         out_specs=(pl.BlockSpec(memory_space=pltpu.HBM),) * 5,
-        scratch_shapes=[dma((5,))],
+        scratch_shapes=[*staged, dma((5,)), dma((5,))],
+        compiler_params=pltpu.CompilerParams(vmem_limit_bytes=64137 * 1024),
     )(*results)
 
 

time: 38.5 us -> 35.8 us (0.930)
  Pallas kernels: 37.7 us -> 35 us
    pallas_call x1, Pallas kernels: 35.4 us -> 32.9 us  [shards(): pl.pallas_call(functools.partial(kernel, cfg), out_shape=(jax.ShapeDtypeS...]
where the time goes in v3:
time: 35.8 us; the launch traced here: 35.6 us
  Pallas kernels  35 us (98%)
  between operations  0.64 us (2%)
    pallas_call x1, Pallas kernels, shards(): pl.pallas_call(functools.partial(kernel, cfg), out_shape=(jax.ShapeDtypeS...  32.9 us
    pallas_call x1, Pallas kernels, shards(): pl.pallas_call(store, out_shape=tuple((jax.ShapeDtypeStruct(one.shape, on...  2.1 us

profile of v3, /device:TPU:0, one launch (start us, length us, event | category | flops | bytes accessed | tf_op | source)
XLA Modules:
  0.0 35.6 jit_solution(14839895897849825756)
XLA Ops:
  0.6 32.9 %shard_map.92 = (bf16[3,2,64,256]{3,2,1,0:T(8,128)(2,1)}, bf16[3,2,64,256]{3,2,1,0:T(8,128)(2,1)}, f32[256,256]{1,0:T(8,128)}, f32[27,8,256]{2,1,0:T(8,128)}, f32[256,256]{1,0:T(8,128)}) custom-call(bf16[3,2,64,256]{3,2,1,0:T(8,128)(2,1)} %x_hbm.1, bf16[256,256]{1,0:T(8,128)(2,1)} %win_hbm.1, bf16[27,8,256]{2,1,0:T(8,128)(2,1)} %wg_hbm.1, ...), custom_call_target="tpu_custom_call" | custom-call | tf_op jit(solution)/shard_map/pallas_call | solution.py:377
  33.5 2.1 %shard_map.93 = (bf16[3,2,64,256]{3,2,1,0:T(8,128)(2,1)}, bf16[3,2,64,256]{3,2,1,0:T(8,128)(2,1)}, f32[256,256]{1,0:T(8,128)}, f32[27,8,256]{2,1,0:T(8,128)}, f32[256,256]{1,0:T(8,128)}) custom-call(bf16[3,2,64,256]{3,2,1,0:T(8,128)(2,1)} %get-tuple-element.10.refs_0_, bf16[3,2,64,256]{3,2,1,0:T(8,128)(2,1)} %get-tuple-element.11.refs_1_, ...), custom_call_target="tpu_custom_call" | custom-call | tf_op jit(solution)/shard_map/pallas_call | solution.py:419

commit v4 on v3

--- a/solution.py
+++ b/solution.py
@@ -295,10 +295,6 @@
 
     grad_out = dot_nn(second.T, cot_ref[...].reshape(cells, chans))
     back_s[0:chans] = grad_out
-    mixed = dot_nn(second, wout_ref[...])
-    out_ref[...] = (x_ref[...].reshape(cells, chans).astype(F32) + mixed).astype(BF).reshape(full)
-    shifted_inner(1)
-    keep[0].start()
 
     gtap[...] = jnp.zeros(gtap.shape, F32)
 
@@ -318,6 +314,10 @@
 
     lax.fori_loop(0, 3, taps, 0)
     sum_start(0, back_s[0:chans], gtap[...].reshape(chans, chans))
+    mixed = dot_nn(second, wout_ref[...])
+    out_ref[...] = (x_ref[...].reshape(cells, chans).astype(F32) + mixed).astype(BF).reshape(full)
+    shifted_inner(1)
+    keep[0].start()
 
     halo_wait(1)
     shifted_edges(1)
@@ -328,10 +328,10 @@
     sig = sigmoid(pre)
     mixed = (back * (sig * (1.0 + pre * (1.0 - sig)))).astype(BF)
     sum_start(1, dot_nn(turned_x[...], mixed))
+    sum_spread(0)
     back_in = dot_nt(mixed, win_ref[...])
     cot32 = cot_ref[...].reshape(cells, chans).astype(F32)
     ig_ref[...] = (cot32 + back_in).astype(BF).reshape(full)
-    sum_spread(0)
     keep[1].start()
     sum_spread(1)
     sum_gather(0)

time: 35.8 us -> 35.7 us (level)
  no operation moved by 1% of the time
where the time goes in v4:
time: 35.7 us; the launch traced here: 35.5 us
  Pallas kernels  34.9 us (98%)
  between operations  0.64 us (2%)
    pallas_call x1, Pallas kernels, shards(): pl.pallas_call(functools.partial(kernel, cfg), out_shape=(jax.ShapeDtypeS...  32.8 us
    pallas_call x1, Pallas kernels, shards(): pl.pallas_call(store, out_shape=tuple((jax.ShapeDtypeStruct(one.shape, on...  2.1 us

profile of v4, /device:TPU:0, one launch (start us, length us, event | category | flops | bytes accessed | tf_op | source)
XLA Modules:
  0.0 35.5 jit_solution(11264459970300217738)
XLA Ops:
  0.6 32.8 %shard_map.92 = (bf16[3,2,64,256]{3,2,1,0:T(8,128)(2,1)}, bf16[3,2,64,256]{3,2,1,0:T(8,128)(2,1)}, f32[256,256]{1,0:T(8,128)}, f32[27,8,256]{2,1,0:T(8,128)}, f32[256,256]{1,0:T(8,128)}) custom-call(bf16[3,2,64,256]{3,2,1,0:T(8,128)(2,1)} %x_hbm.1, bf16[256,256]{1,0:T(8,128)(2,1)} %win_hbm.1, bf16[27,8,256]{2,1,0:T(8,128)(2,1)} %wg_hbm.1, ...), custom_call_target="tpu_custom_call" | custom-call | tf_op jit(solution)/shard_map/pallas_call | solution.py:377
  33.4 2.1 %shard_map.93 = (bf16[3,2,64,256]{3,2,1,0:T(8,128)(2,1)}, bf16[3,2,64,256]{3,2,1,0:T(8,128)(2,1)}, f32[256,256]{1,0:T(8,128)}, f32[27,8,256]{2,1,0:T(8,128)}, f32[256,256]{1,0:T(8,128)}) custom-call(bf16[3,2,64,256]{3,2,1,0:T(8,128)(2,1)} %get-tuple-element.10.refs_0_, bf16[3,2,64,256]{3,2,1,0:T(8,128)(2,1)} %get-tuple-element.11.refs_1_, ...), custom_call_target="tpu_custom_call" | custom-call | tf_op jit(solution)/shard_map/pallas_call | solution.py:419
